TPU v7x, 128 devices: a whole 4x4x4 slice. The times are simulated.
128 devices in a mesh: ep: 16 (over x, z), tp: 8 (over y, core).
Axes of the slice: x: 4, y: 4, z: 4, core: 2. Of those that a mesh axis runs over, the one named last changes fastest.
Arguments:
- tokens: bfloat16 [2048, 4096], P('ep', 'tp'), may hold values from -6 to 6
- out_grad: bfloat16 [2048, 4096], P('ep', 'tp'), may hold values from -6 to 6
- routes: int32 [2048, 4], P('ep'), may hold values from 0 to 15, all different within a row; in each aligned block of 128 rows (0 to 127, 128 to 255, ...) at most 64 rows name the same one
- probs: bfloat16 [2048, 4], P('ep'), may hold values from 0.019897461 to 0.59765625
- w_in: bfloat16 [16, 2, 1536, 4096], P('ep', None, 'tp'), as said below
- w_out: bfloat16 [16, 1536, 4096], P('ep', 'tp'), as said below
Outputs:
- in_grad: bfloat16 [2048, 4096], P('ep', 'tp')
- grad_in: bfloat16 [16, 2, 1536, 4096], P('ep', None, 'tp')
- grad_out: bfloat16 [16, 1536, 4096], P('ep', 'tp')
Inputs may be any that keep to these rules, and one draw needn't show every extreme that they name: `routes`: each token names 4 different copies; within the tokens of one device (aligned blocks of 128 tokens) no copy is named more than 64 times, a bound that some block reaches. `w_in`: copies c and c + 8 hold equal weights. `w_out`: copies c and c + 8 hold equal weights.
All inputs are finite; a program needn't handle non-finite values.
Results may differ from a plain program's by a relative error of at most 0.02.
Values may be sent and summed in bfloat16 or wider, within the bound.
A program may use at most 128 MiB of HBM per device.

v0:
```python
import jax
import jax.numpy as jnp
from jax import lax
from jax.sharding import PartitionSpec as P


def partner(block, axis, apart):
    count = lax.axis_size(axis)
    route = []
    for low in range(count):
        high = low | 1 << apart
        if high != low and high < count:
            route += [(low, high), (high, low)]
    return lax.ppermute(block, axis, route)


def slot_tables(block_routes, copies, cap):
    flat = block_routes.reshape(-1)
    nrows = flat.shape[0]
    onehot = (flat[:, None] == jnp.arange(copies, dtype=jnp.int32)[None, :]).astype(jnp.int32)
    ranks = jnp.sum((jnp.cumsum(onehot, axis=0) - 1) * onehot, axis=1)
    slot = flat * cap + ranks
    source = (
        jnp.full((copies * cap,), nrows, jnp.int32).at[slot].set(jnp.arange(nrows, dtype=jnp.int32))
    )
    return (slot, source)


def body(tokens, out_grad, routes, probs, w_in, w_out):
    n_ep = lax.axis_size("ep")
    tok_dev, top = routes.shape
    nrows = tok_dev * top
    cap = 2 * nrows // n_ep
    slot, source = slot_tables(routes, n_ep, cap)
    valid = source < nrows
    local = jnp.minimum(source, nrows - 1)
    tok_index = local // top
    scale = jnp.where(valid, probs.reshape(-1)[local].astype(jnp.float32), 0.0)[:, None]
    full_x, full_g = (
        lax.all_gather(tokens, "tp", axis=1, tiled=True),
        lax.all_gather(out_grad, "tp", axis=1, tiled=True),
    )
    packed_x = jnp.where(valid[:, None], full_x[tok_index], jnp.zeros((), jnp.bfloat16))
    packed_g = (scale * full_g[tok_index].astype(jnp.float32)).astype(jnp.bfloat16)
    width = full_x.shape[1]
    send_x = packed_x.reshape(n_ep, cap, width)
    send_g = packed_g.reshape(n_ep, cap, width)
    recv_x, recv_g = (
        lax.all_to_all(send_x, "ep", split_axis=0, concat_axis=0, tiled=True),
        lax.all_to_all(send_g, "ep", split_axis=0, concat_axis=0, tiled=True),
    )
    width = recv_x.shape[2]
    rows_x = recv_x.reshape(n_ep * cap, width)
    rows_g = recv_g.reshape(n_ep * cap, width)
    w_gate = w_in[0, 0]
    w_up = w_in[0, 1]
    w_down = w_out[0]
    contract_last = (((1,), (1,)), ((), ()))
    a = lax.dot_general(rows_x, w_gate, contract_last, preferred_element_type=jnp.float32)
    b = lax.dot_general(rows_x, w_up, contract_last, preferred_element_type=jnp.float32)
    sig = jax.nn.sigmoid(a)
    silu = a * sig
    hidden = (silu * b).astype(jnp.bfloat16)
    dh = lax.dot_general(rows_g, w_down, contract_last, preferred_element_type=jnp.float32)
    da = (dh * b * sig * (1.0 + a * (1.0 - sig))).astype(jnp.bfloat16)
    db = (dh * silu).astype(jnp.bfloat16)
    partial_rows = jnp.dot(da, w_gate, preferred_element_type=jnp.float32)
    partial_rows = partial_rows + jnp.dot(db, w_up, preferred_element_type=jnp.float32)
    summed = lax.psum_scatter(
        partial_rows.reshape(n_ep, cap, width).astype(jnp.bfloat16),
        "tp",
        scatter_dimension=2,
        tiled=True,
    )
    back = lax.all_to_all(summed, "ep", split_axis=0, concat_axis=0, tiled=True)
    picked = back.reshape(n_ep * cap, back.shape[2])[slot]
    in_grad = jnp.sum(
        picked.astype(jnp.float32).reshape(tok_dev, top, back.shape[2]), axis=1
    ).astype(jnp.bfloat16)
    contract_rows = (((0,), (0,)), ((), ()))
    own_in = jnp.stack(
        [
            lax.dot_general(da, rows_x, contract_rows, preferred_element_type=jnp.float32),
            lax.dot_general(db, rows_x, contract_rows, preferred_element_type=jnp.float32),
        ]
    ).astype(jnp.bfloat16)[None]
    own_out = lax.dot_general(
        hidden, rows_g, contract_rows, preferred_element_type=jnp.float32
    ).astype(jnp.bfloat16)[None]
    half_bit = n_ep.bit_length() - 2
    other_in, other_out = partner((own_in, own_out), "ep", half_bit)
    grad_in = (own_in.astype(jnp.float32) + other_in.astype(jnp.float32)).astype(jnp.bfloat16)
    grad_out = (own_out.astype(jnp.float32) + other_out.astype(jnp.float32)).astype(jnp.bfloat16)
    return (in_grad, grad_in, grad_out)


def solution(mesh):
    return jax.shard_map(
        body,
        mesh=mesh,
        in_specs=(
            P("ep", "tp"),
            P("ep", "tp"),
            P("ep", None),
            P("ep", None),
            P("ep", None, "tp", None),
            P("ep", "tp", None),
        ),
        out_specs=(P("ep", "tp"), P("ep", None, "tp", None), P("ep", "tp", None)),
        check_vma=False,
    )
```

profile of v0, /device:TPU:0, one launch (start us, length us, event | category | flops | bytes accessed | tf_op | source)
XLA Modules:
  0.0 534.7 jit_solution(16174911186118901653)
XLA Ops:
  7.2 0.0 copy-start
  7.2 0.0 all-gather.5.cloned.1.call-start
  7.2 0.7 all-gather.5.cloned.1.call-update
  7.9 0.8 copy.10
  8.7 0.1 eq.29
  8.8 0.1 eq.25
  8.9 1.2 reduce-window.6
  10.1 0.2 slice_reduce_fusion
  10.3 0.7 broadcast_multiply_fusion
  11.0 0.1 copy.9
  11.2 0.1 mul.53
  11.3 0.8 copy.13
  12.1 0.1 reshape.144
  12.2 0.1 fusion.20
  12.3 2.4 scatter_custom_fusion
  14.8 6.8 %gather_fusion = bf16[1024]{0:T(1024)(128)(2,1)S(1)} fusion(bf16[512]{0:T(512)(128)(2,1)S(1)} %reshape.144, s32[1024]{0:T(1024)S(1)} %get-tuple-element.7), kind=kCustom, calls=%fused_computation | custom fusion | bytes 8192 | tf_op jit(solution)/shard_map/gather | solution.py:38
  21.6 0.1 broadcast_in_dim.35
  21.7 13.9 %all-gather.5.cloned.1.call-done = bf16[128,4096]{1,0:T(8,128)(2,1)} async-done(((bf16[128,512]{1,0:T(8,128)(2,1)}), bf16[128,4096]{1,0:T(8,128)(2,1)}) %all-gather.5.cloned.1.call-update) | async-done | bytes 1048592 | tf_op jit(solution)/shard_map/all_gather | solution.py:40
  35.6 16.4 %gather_fusion.2 = bf16[1024,4096]{1,0:T(8,128)(2,1)} fusion(bf16[128,4096]{1,0:T(8,128)(2,1)} %all-gather.5.cloned.1.call-done, s32[1024]{0:T(1024)S(1)} %get-tuple-element.8), kind=kCustom, calls=%fused_computation.2 | custom fusion | bytes 16781312 | tf_op jit(solution)/shard_map/gather | solution.py:43
  52.0 7.2 %broadcast_select_fusion = bf16[16,64,4096]{2,1,0:T(8,128)(2,1)} fusion(bf16[16,64,4096]{2,1,0:T(8,128)(2,1)} %bitcast.56, pred[16,64]{1,0:T(8,128)(4,1)S(1)} %broadcast_in_dim.35), kind=kLoop, calls=%fused_computation.8 | loop fusion | flops 4194304 | bytes 16778240 | tf_op jit(solution)/shard_map/jit(_where)/select_n | solution.py:43
  59.2 7.0 %all-to-all-start.1 = ((bf16[16,64,4096]{2,1,0:T(8,128)(2,1)}), bf16[16,64,4096]{2,1,0:T(8,128)(2,1)}, u32[]{:S(2)}, u32[]{:S(2)}) async-start(bf16[16,64,4096]{2,1,0:T(8,128)(2,1)} %broadcast_select_fusion), calls=%async_computation.1 | async-start | bytes 16777216 | tf_op jit(solution)/shard_map/all_to_all | solution.py:49
  66.3 0.0 all-gather.3.cloned.1.call-start
  66.3 0.7 all-gather.3.cloned.1.call-update
  67.0 0.1 mul.55
  67.1 25.2 %all-gather.3.cloned.1.call-done = bf16[128,4096]{1,0:T(8,128)(2,1)} async-done(((bf16[128,512]{1,0:T(8,128)(2,1)}), bf16[128,4096]{1,0:T(8,128)(2,1)}) %all-gather.3.cloned.1.call-update) | async-done | bytes 1048592 | tf_op jit(solution)/shard_map/all_gather | solution.py:41
  92.3 16.4 %gather_fusion.1 = bf16[1024,4096]{1,0:T(8,128)(2,1)} fusion(bf16[128,4096]{1,0:T(8,128)(2,1)} %all-gather.3.cloned.1.call-done, s32[1024]{0:T(1024)S(1)} %get-tuple-element.8), kind=kCustom, calls=%fused_computation.1 | custom fusion | bytes 16781312 | tf_op jit(solution)/shard_map/gather | solution.py:44
  108.7 10.0 %fusion = bf16[16,64,4096]{2,1,0:T(8,128)(2,1)} fusion(bf16[16,64,4096]{2,1,0:T(8,128)(2,1)} %bitcast.57, f32[16,64]{1,0:T(8,128)S(1)} %mul.55), kind=kLoop, calls=%fused_computation.6 | loop fusion | flops 12582912 | bytes 16781312 | tf_op jit(solution)/shard_map/convert_element_type | solution.py:44
  118.7 93.8 %all-to-all-done.1 = bf16[16,64,4096]{2,1,0:T(8,128)(2,1)} async-done(((bf16[16,64,4096]{2,1,0:T(8,128)(2,1)}), bf16[16,64,4096]{2,1,0:T(8,128)(2,1)}, u32[]{:S(2)}, u32[]{:S(2)}) %all-to-all-start.1) | async-done | bytes 8388640 | tf_op jit(solution)/shard_map/all_to_all | solution.py:49
  212.5 11.8 %all-to-all-start = ((bf16[16,64,4096]{2,1,0:T(8,128)(2,1)}), bf16[16,64,4096]{2,1,0:T(8,128)(2,1)}, u32[]{:S(2)}, u32[]{:S(2)}) async-start(bf16[16,64,4096]{2,1,0:T(8,128)(2,1)} %fusion), calls=%async_computation | async-start | bytes 16777216 | tf_op jit(solution)/shard_map/all_to_all | solution.py:50
  224.3 0.2 reduce-scatter.2.cloned.1.call-start
  224.5 0.0 copy-start.3
  224.5 6.8 %fusion.6 = f32[1024,192]{0,1:T(8,128)S(1)} fusion(bf16[1024,4096]{1,0:T(8,128)(2,1)} %bitcast.7, bf16[1,2,192,4096]{3,2,1,0:T(8,128)(2,1)} %param.10), kind=kOutput, calls=%fused_computation.20 | convolution fusion | flops 1610612736 | bytes 10747904 | tf_op jit(solution)/shard_map/dot_general | solution.py:59
  231.4 0.0 copy-done.3
  231.4 7.2 %fusion.9 = f32[1024,192]{0,1:T(8,128)} fusion(bf16[1024,4096]{1,0:T(8,128)(2,1)} %bitcast.7, bf16[1,2,192,4096]{3,2,1,0:T(8,128)(2,1)S(1)} %copy-done.3), kind=kOutput, calls=%fused_computation.23 | convolution fusion | flops 1610612736 | bytes 10747904 | tf_op jit(solution)/shard_map/dot_general | solution.py:60
  238.5 119.4 %all-to-all-done = bf16[16,64,4096]{2,1,0:T(8,128)(2,1)} async-done(((bf16[16,64,4096]{2,1,0:T(8,128)(2,1)}), bf16[16,64,4096]{2,1,0:T(8,128)(2,1)}, u32[]{:S(2)}, u32[]{:S(2)}) %all-to-all-start) | async-done | bytes 8388640 | tf_op jit(solution)/shard_map/all_to_all | solution.py:50
  357.9 0.0 copy-done
  357.9 0.0 copy-start.4
  357.9 6.7 %multiply_convert_fusion.1 = (bf16[1024,192]{0,1:T(8,128)(2,1)S(1)}, bf16[1024,192]{0,1:T(8,128)(2,1)S(1)}) fusion(f32[1024,192]{0,1:T(8,128)S(1)} %fusion.6, f32[1024,192]{0,1:T(8,128)} %fusion.9, bf16[1024,4096]{1,0:T(8,128)(2,1)} %bitcast.4, bf16[1,192,4096]{2,1,0:T(8,128)(2,1)S(1)} %copy-done), kind=kOutput, calls=%fused_computation.32 | convolution fusion | flops 1613168640 | bytes 12320768 | tf_op jit(solution)/shard_map/dot_general | solution.py:64
  364.6 0.0 copy-done.4
  364.6 8.1 %fusion.4 = f32[1024,4096]{1,0:T(8,128)} fusion(bf16[1024,192]{0,1:T(8,128)(2,1)S(1)} %get-tuple-element.6, bf16[1,2,192,4096]{3,2,1,0:T(8,128)(2,1)S(1)} %copy-done.4), kind=kOutput, calls=%fused_computation.18 | convolution fusion | flops 1610612736 | bytes 18743296 | tf_op jit(solution)/shard_map/dot_general | solution.py:67
  372.8 11.4 %add_convert_fusion = bf16[1024,4096]{1,0:T(8,128)(2,1)} fusion(f32[1024,4096]{1,0:T(8,128)} %fusion.4, bf16[1024,192]{0,1:T(8,128)(2,1)S(1)} %get-tuple-element.5, bf16[1,2,192,4096]{3,2,1,0:T(8,128)(2,1)S(1)} %copy-done.4), kind=kOutput, calls=%fused_computation.7 | convolution fusion | flops 1619001344 | bytes 27131904 | tf_op jit(solution)/shard_map/dot_general | solution.py:68
  384.2 0.0 reduce-scatter.2.cloned.1.call-update
  384.2 5.4 %fusion.1 = bf16[1,1,192,4096]{3,2,1,0:T(8,128)(2,1)S(1)} fusion(bf16[1024,192]{0,1:T(8,128)(2,1)S(1)} %get-tuple-element.6, bf16[1024,4096]{1,0:T(8,128)(2,1)} %bitcast.7), kind=kOutput, calls=%fused_computation.13 | convolution fusion | flops 1611399168 | bytes 10354688 | tf_op jit(solution)/shard_map/dot_general | solution.py:83
  389.6 0.0 copy-start.1
  389.7 5.8 %fusion.2 = bf16[1,1,192,4096]{3,2,1,0:T(8,128)(2,1)S(1)} fusion(bf16[1024,192]{0,1:T(8,128)(2,1)S(1)} %get-tuple-element.5, bf16[1024,4096]{1,0:T(8,128)(2,1)} %bitcast.7), kind=kOutput, calls=%fused_computation.14 | convolution fusion | flops 1611399168 | bytes 10354688 | tf_op jit(solution)/shard_map/dot_general | solution.py:84
  395.4 0.0 copy-done.1
  395.4 0.0 copy-start.2
  395.4 0.0 copy-start.5
  395.4 1.9 pad_maximum_fusion
  397.4 0.2 copy-done.2
  397.6 0.0 collective-permute-start
  397.6 0.0 copy-done.5
  397.6 5.3 fusion.3
  402.9 3.7 collective-permute-start.1
  406.6 92.6 %collective-permute-done.1 = bf16[1,192,4096]{2,1,0:T(8,128)(2,1)S(1)} collective-permute-done((bf16[1,192,4096]{2,1,0:T(8,128)(2,1)S(1)}, bf16[1,192,4096]{2,1,0:T(8,128)(2,1)S(1)}, u32[]{:S(2)}, u32[]{:S(2)}) %collective-permute-start.1) | collective-permute-done | bytes 1572896 | tf_op jit(solution)/shard_map/ppermute | solution.py:14
  499.2 1.7 add_convert_fusion.2
  500.9 0.0 reduce-scatter.2.cloned.1.call-done
  500.9 9.9 %all-to-all-start.2 = ((bf16[16,64,512]{2,1,0:T(8,128)(2,1)}), bf16[16,64,512]{2,1,0:T(8,128)(2,1)S(1)}, u32[]{:S(2)}, u32[]{:S(2)}) async-start(bf16[16,64,512]{2,1,0:T(8,128)(2,1)} %reduce-scatter.2.cloned.1.call-done), calls=%async_computation.3 | async-start | bytes 2097152 | tf_op jit(solution)/shard_map/all_to_all | solution.py:75
  510.8 0.0 collective-permute-done
  510.8 5.8 %add_convert_fusion.1 = bf16[1,2,192,4096]{3,2,1,0:T(8,128)(2,1)} fusion(bf16[1,2,192,4096]{3,2,1,0:T(8,128)(2,1)} %collective-permute-done, bf16[1,1,192,4096]{3,2,1,0:T(8,128)(2,1)} %copy-done.2, bf16[1,1,192,4096]{3,2,1,0:T(8,128)(2,1)} %copy-done.1), kind=kLoop, calls=%fused_computation.9 | loop fusion | flops 7864320 | bytes 9437184 | tf_op jit(solution)/shard_map/convert_element_type | solution.py:92
  516.6 8.2 %all-to-all-done.2 = bf16[16,64,512]{2,1,0:T(8,128)(2,1)S(1)} async-done(((bf16[16,64,512]{2,1,0:T(8,128)(2,1)}), bf16[16,64,512]{2,1,0:T(8,128)(2,1)S(1)}, u32[]{:S(2)}, u32[]{:S(2)}) %all-to-all-start.2) | async-done | bytes 1048608 | tf_op jit(solution)/shard_map/all_to_all | solution.py:75
  524.7 2.0 gather_fusion.3
  526.7 0.1 gather.21
  526.8 1.3 reduce_sum.25
  (8 shorter events, 0.1 us)
Async XLA Ops:
  7.2 350.7 %copy-start = (bf16[1,192,4096]{2,1,0:T(8,128)(2,1)S(1)}, bf16[1,192,4096]{2,1,0:T(8,128)(2,1)}, u32[]{:S(2)}) copy-start(bf16[1,192,4096]{2,1,0:T(8,128)(2,1)} %param.11) | copy-start | bytes 4718596
  7.2 28.4 %all-gather.5.cloned.1.call-start = ((), (), s32[]{:S(2)}) async-start(), calls=%async_computation.5 | async-start | bytes 1179648 | tf_op jit(solution)/shard_map/all_gather | solution.py:40
  59.2 153.3 %all-to-all-start.1 = ((bf16[16,64,4096]{2,1,0:T(8,128)(2,1)}), bf16[16,64,4096]{2,1,0:T(8,128)(2,1)}, u32[]{:S(2)}, u32[]{:S(2)}) async-start(bf16[16,64,4096]{2,1,0:T(8,128)(2,1)} %broadcast_select_fusion), calls=%async_computation.1 | async-start | bytes 16777216 | tf_op jit(solution)/shard_map/all_to_all | solution.py:49
  66.3 26.0 %all-gather.3.cloned.1.call-start = ((), (), s32[]{:S(2)}) async-start(), calls=%async_computation.4 | async-start | bytes 1179648 | tf_op jit(solution)/shard_map/all_gather | solution.py:41
  212.5 145.4 %all-to-all-start = ((bf16[16,64,4096]{2,1,0:T(8,128)(2,1)}), bf16[16,64,4096]{2,1,0:T(8,128)(2,1)}, u32[]{:S(2)}, u32[]{:S(2)}) async-start(bf16[16,64,4096]{2,1,0:T(8,128)(2,1)} %fusion), calls=%async_computation | async-start | bytes 16777216 | tf_op jit(solution)/shard_map/all_to_all | solution.py:50
  224.3 276.6 %reduce-scatter.2.cloned.1.call-start = ((), (), s32[]{:S(2)}) async-start(), calls=%async_computation.6 | async-start | bytes 9437184 | tf_op jit(solution)/shard_map/reduce_scatter | solution.py:69
  224.5 6.9 %copy-start.3 = (bf16[1,2,192,4096]{3,2,1,0:T(8,128)(2,1)S(1)}, bf16[1,2,192,4096]{3,2,1,0:T(8,128)(2,1)}, u32[]{:S(2)}) copy-start(bf16[1,2,192,4096]{3,2,1,0:T(8,128)(2,1)} %param.10) | copy-start | bytes 9437188
  357.9 6.7 %copy-start.4 = (bf16[1,2,192,4096]{3,2,1,0:T(8,128)(2,1)S(1)}, bf16[1,2,192,4096]{3,2,1,0:T(8,128)(2,1)}, u32[]{:S(2)}) copy-start(bf16[1,2,192,4096]{3,2,1,0:T(8,128)(2,1)} %param.10) | copy-start | bytes 9437188
  389.6 5.8 %copy-start.1 = (bf16[1,1,192,4096]{3,2,1,0:T(8,128)(2,1)}, bf16[1,1,192,4096]{3,2,1,0:T(8,128)(2,1)S(1)}, u32[]{:S(2)}) copy-start(bf16[1,1,192,4096]{3,2,1,0:T(8,128)(2,1)S(1)} %fusion.1) | copy-start | bytes 4718596
  395.4 2.2 copy-start.2
  395.4 2.2 copy-start.5
  397.6 113.2 %collective-permute-start = (bf16[1,2,192,4096]{3,2,1,0:T(8,128)(2,1)}, bf16[1,2,192,4096]{3,2,1,0:T(8,128)(2,1)}, u32[]{:S(2)}, u32[]{:S(2)}) collective-permute-start(bf16[1,2,192,4096]{3,2,1,0:T(8,128)(2,1)} %pad_maximum_fusion), channel_id=1, source_target_pairs={{0,64},{64,0},{8,72},{72,8},{16,80},{80,16},{24,88},{88,24},{32,96... | collective-permute-start | bytes 9437192 | tf_op jit(solution)/shard_map/ppermute | solution.py:14
  402.9 96.3 %collective-permute-start.1 = (bf16[1,192,4096]{2,1,0:T(8,128)(2,1)S(1)}, bf16[1,192,4096]{2,1,0:T(8,128)(2,1)S(1)}, u32[]{:S(2)}, u32[]{:S(2)}) collective-permute-start(bf16[1,192,4096]{2,1,0:T(8,128)(2,1)S(1)} %fusion.3), channel_id=1, source_target_pairs={{0,64},{64,0},{8,72},{72,8},{16,80},{80,16},{24,88},{88,24},{32,96... | collective-permute-start | bytes 4718600 | tf_op jit(solution)/shard_map/ppermute | solution.py:14
  500.9 23.9 %all-to-all-start.2 = ((bf16[16,64,512]{2,1,0:T(8,128)(2,1)}), bf16[16,64,512]{2,1,0:T(8,128)(2,1)S(1)}, u32[]{:S(2)}, u32[]{:S(2)}) async-start(bf16[16,64,512]{2,1,0:T(8,128)(2,1)} %reduce-scatter.2.cloned.1.call-done), calls=%async_computation.3 | async-start | bytes 2097152 | tf_op jit(solution)/shard_map/all_to_all | solution.py:75
Sparse Core Ops, SparseCore 0:
  9.7 25.8 all-gather.4
  68.8 23.4 all-gather.2
  384.3 54.3 reduce-scatter.1
where the time goes:
time: 535 us
  waiting for transfers between devices  354 us (66%)
  matrix products  56.7 us (11%)
  local copies, waits for them, and re-layouts  47 us (9%)
  starting transfers between devices  32.6 us (6%)
  other arithmetic  30 us (6%)
  between operations  14 us (3%)
    all_to_all x1, waiting for transfers between devices, body(): lax.all_to_all(send_g, 'ep', split_axis=0, concat_axis=0, tiled=True)  119 us
    all_to_all x1, waiting for transfers between devices, body(): lax.all_to_all(send_x, 'ep', split_axis=0, concat_axis=0, tiled=True)  93.8 us
    ppermute x2, waiting for transfers between devices, partner(): return lax.ppermute(block, axis, route)  92.6 us
    all_gather x1, waiting for transfers between devices, body(): lax.all_gather(out_grad, 'tp', axis=1, tiled=True)  25.2 us
    gather x1, local copies, waits for them, and re-layouts, body(): full_g[tok_index].astype(jnp.float32)  16.4 us
    gather x1, local copies, waits for them, and re-layouts, body(): full_x[tok_index]  16.4 us
    all_gather x1, waiting for transfers between devices, body(): lax.all_gather(tokens, 'tp', axis=1, tiled=True)  13.9 us
    all_to_all x1, starting transfers between devices, body(): lax.all_to_all(send_g, 'ep', split_axis=0, concat_axis=0, tiled=True)  11.8 us
  transfers between devices with their start and end apart: 8, of which 6 were waited for; matrix products, arithmetic and copies ran while one was open for 15% of the time, Pallas kernels for 0%

commit v1 on v0

--- a/solution.py
+++ b/solution.py
@@ -37,7 +37,9 @@
     tok_index = local // top
     scale = jnp.where(valid, probs.reshape(-1)[local].astype(jnp.float32), 0.0)[:, None]
     full_x, full_g = (
-        lax.all_gather(tokens, "tp", axis=1, tiled=True),
+        jnp.concatenate(
+            lax.all_to_all(jnp.stack([tokens] * lax.axis_size("tp")), "tp", 0, 0), axis=1
+        ),
         lax.all_gather(out_grad, "tp", axis=1, tiled=True),
     )
     packed_x = jnp.where(valid[:, None], full_x[tok_index], jnp.zeros((), jnp.bfloat16))

time: 535 us -> 518 us (0.968)
  the two profiles are of different devices: /device:TPU:0 before, /device:TPU:16 now
where the time goes in v1:
time: 518 us; the launch traced here: 517 us
  waiting for transfers between devices  341 us (66%)
  matrix products  56.8 us (11%)
  local copies, waits for them, and re-layouts  41.5 us (8%)
  starting transfers between devices  33.8 us (7%)
  other arithmetic  29.3 us (6%)
  between operations  14.3 us (3%)
    all_to_all x1, waiting for transfers between devices, body(): lax.all_to_all(send_g, 'ep', split_axis=0, concat_axis=0, tiled=True)  119 us
    all_to_all x1, waiting for transfers between devices, body(): lax.all_to_all(send_x, 'ep', split_axis=0, concat_axis=0, tiled=True)  94 us
    ppermute x2, waiting for transfers between devices, partner(): return lax.ppermute(block, axis, route)  92.2 us
    all_gather x1, waiting for transfers between devices, body(): lax.all_gather(out_grad, 'tp', axis=1, tiled=True)  26 us
    gather x1, local copies, waits for them, and re-layouts, body(): full_g[tok_index].astype(jnp.float32)  16.4 us
    dot_general x1, matrix products, body(): jnp.dot(db, w_up, preferred_element_type=jnp.float32)  11.4 us
  transfers between devices with their start and end apart: 8, of which 6 were waited for; matrix products, arithmetic and copies ran while one was open for 15% of the time, Pallas kernels for 0%

profile of v1, /device:TPU:16, one launch (start us, length us, event | category | flops | bytes accessed | tf_op | source)
XLA Modules:
  0.0 517.0 jit_solution(12348843069956194823)
XLA Ops:
  7.2 0.0 copy-start
  7.2 0.0 copy-start.6
  7.2 0.0 copy-start.7
  7.2 2.1 stack.8
  9.3 4.8 all-to-all-start.1
  14.1 0.0 copy-done.6
  14.1 0.1 copy.15
  14.2 0.1 eq.29
  14.3 0.1 eq.25
  14.4 1.2 reduce-window.6
  15.6 0.2 slice_reduce_fusion
  15.8 0.1 copy.14
  16.0 0.1 mul.53
  16.1 0.0 copy-done.7
  16.1 0.1 copy.18
  16.2 0.1 reshape.152
  16.3 0.1 fusion.20
  16.5 2.4 scatter_custom_fusion
  18.9 6.8 %gather_fusion = bf16[1024]{0:T(1024)(128)(2,1)S(1)} fusion(bf16[512]{0:T(512)(128)(2,1)S(1)} %reshape.152, s32[1024]{0:T(1024)S(1)} %get-tuple-element.7), kind=kCustom, calls=%fused_computation | custom fusion | bytes 8192 | tf_op jit(solution)/shard_map/gather | solution.py:38
  25.8 0.1 broadcast_in_dim.35
  25.8 1.1 all-to-all-done.1
  26.9 1.0 copy-done.3
  27.9 1.3 copy.21
  29.2 7.8 %gather_fusion.2 = bf16[1024,4096]{1,0:T(8,128)(2,1)} fusion(bf16[128,4096]{1,0:T(8,128)(2,1)S(1)} %bitcast.58, s32[1024]{0:T(1024)S(1)} %get-tuple-element.8), kind=kCustom, calls=%fused_computation.2 | custom fusion | bytes 16781312 | tf_op jit(solution)/shard_map/gather | solution.py:45
  37.0 7.2 %broadcast_select_fusion = bf16[16,64,4096]{2,1,0:T(8,128)(2,1)} fusion(bf16[16,64,4096]{2,1,0:T(8,128)(2,1)} %bitcast.60, pred[16,64]{1,0:T(8,128)(4,1)S(1)} %broadcast_in_dim.35), kind=kLoop, calls=%fused_computation.8 | loop fusion | flops 4194304 | bytes 16778240 | tf_op jit(solution)/shard_map/jit(_where)/select_n | solution.py:45
  44.2 7.9 %all-to-all-start.2 = ((bf16[16,64,4096]{2,1,0:T(8,128)(2,1)}), bf16[16,64,4096]{2,1,0:T(8,128)(2,1)}, u32[]{:S(2)}, u32[]{:S(2)}) async-start(bf16[16,64,4096]{2,1,0:T(8,128)(2,1)} %broadcast_select_fusion), calls=%async_computation.2 | async-start | bytes 16777216 | tf_op jit(solution)/shard_map/all_to_all | solution.py:51
  52.1 0.0 all-gather.2.cloned.1.call-start
  52.2 0.7 all-gather.2.cloned.1.call-update
  52.9 0.1 mul.55
  53.0 26.0 %all-gather.2.cloned.1.call-done = bf16[128,4096]{1,0:T(8,128)(2,1)} async-done(((bf16[128,512]{1,0:T(8,128)(2,1)}), bf16[128,4096]{1,0:T(8,128)(2,1)}) %all-gather.2.cloned.1.call-update) | async-done | bytes 1048592 | tf_op jit(solution)/shard_map/all_gather | solution.py:43
  79.0 16.4 %gather_fusion.1 = bf16[1024,4096]{1,0:T(8,128)(2,1)} fusion(bf16[128,4096]{1,0:T(8,128)(2,1)} %all-gather.2.cloned.1.call-done, s32[1024]{0:T(1024)S(1)} %get-tuple-element.8), kind=kCustom, calls=%fused_computation.1 | custom fusion | bytes 16781312 | tf_op jit(solution)/shard_map/gather | solution.py:46
  95.4 10.0 %fusion = bf16[16,64,4096]{2,1,0:T(8,128)(2,1)} fusion(bf16[16,64,4096]{2,1,0:T(8,128)(2,1)} %bitcast.61, f32[16,64]{1,0:T(8,128)S(1)} %mul.55), kind=kLoop, calls=%fused_computation.6 | loop fusion | flops 12582912 | bytes 16781312 | tf_op jit(solution)/shard_map/convert_element_type | solution.py:46
  105.4 94.0 %all-to-all-done.2 = bf16[16,64,4096]{2,1,0:T(8,128)(2,1)} async-done(((bf16[16,64,4096]{2,1,0:T(8,128)(2,1)}), bf16[16,64,4096]{2,1,0:T(8,128)(2,1)}, u32[]{:S(2)}, u32[]{:S(2)}) %all-to-all-start.2) | async-done | bytes 8388640 | tf_op jit(solution)/shard_map/all_to_all | solution.py:51
  199.4 8.4 %all-to-all-start = ((bf16[16,64,4096]{2,1,0:T(8,128)(2,1)}), bf16[16,64,4096]{2,1,0:T(8,128)(2,1)}, u32[]{:S(2)}, u32[]{:S(2)}) async-start(bf16[16,64,4096]{2,1,0:T(8,128)(2,1)} %fusion), calls=%async_computation | async-start | bytes 16777216 | tf_op jit(solution)/shard_map/all_to_all | solution.py:52
  207.8 0.2 reduce-scatter.2.cloned.1.call-start
  208.0 0.0 copy-start.4
  208.0 6.8 %fusion.6 = f32[1024,192]{0,1:T(8,128)S(1)} fusion(bf16[1024,4096]{1,0:T(8,128)(2,1)} %bitcast.8, bf16[1,2,192,4096]{3,2,1,0:T(8,128)(2,1)} %param.10), kind=kOutput, calls=%fused_computation.20 | convolution fusion | flops 1610612736 | bytes 10747904 | tf_op jit(solution)/shard_map/dot_general | solution.py:61
  214.9 0.0 copy-done.4
  214.9 7.2 %fusion.9 = f32[1024,192]{0,1:T(8,128)} fusion(bf16[1024,4096]{1,0:T(8,128)(2,1)} %bitcast.8, bf16[1,2,192,4096]{3,2,1,0:T(8,128)(2,1)S(1)} %copy-done.4), kind=kOutput, calls=%fused_computation.23 | convolution fusion | flops 1610612736 | bytes 10747904 | tf_op jit(solution)/shard_map/dot_general | solution.py:62
  222.0 119.4 %all-to-all-done = bf16[16,64,4096]{2,1,0:T(8,128)(2,1)} async-done(((bf16[16,64,4096]{2,1,0:T(8,128)(2,1)}), bf16[16,64,4096]{2,1,0:T(8,128)(2,1)}, u32[]{:S(2)}, u32[]{:S(2)}) %all-to-all-start) | async-done | bytes 8388640 | tf_op jit(solution)/shard_map/all_to_all | solution.py:52
  341.5 0.0 copy-done
  341.5 6.7 %multiply_convert_fusion.1 = (bf16[1024,192]{0,1:T(8,128)(2,1)S(1)}, bf16[1024,192]{0,1:T(8,128)(2,1)S(1)}) fusion(f32[1024,192]{0,1:T(8,128)S(1)} %fusion.6, f32[1024,192]{0,1:T(8,128)} %fusion.9, bf16[1024,4096]{1,0:T(8,128)(2,1)} %bitcast.4, bf16[1,192,4096]{2,1,0:T(8,128)(2,1)S(1)} %copy-done), kind=kOutput, calls=%fused_computation.32 | convolution fusion | flops 1613168640 | bytes 12320768 | tf_op jit(solution)/shard_map/dot_general | solution.py:66
  348.2 0.0 copy-done.5
  348.2 8.1 %fusion.4 = f32[1024,4096]{1,0:T(8,128)} fusion(bf16[1024,192]{0,1:T(8,128)(2,1)S(1)} %get-tuple-element.6, bf16[1,2,192,4096]{3,2,1,0:T(8,128)(2,1)S(1)} %copy-done.5), kind=kOutput, calls=%fused_computation.18 | convolution fusion | flops 1610612736 | bytes 18743296 | tf_op jit(solution)/shard_map/dot_general | solution.py:69
  356.4 11.4 %add_convert_fusion = bf16[1024,4096]{1,0:T(8,128)(2,1)} fusion(f32[1024,4096]{1,0:T(8,128)} %fusion.4, bf16[1024,192]{0,1:T(8,128)(2,1)S(1)} %get-tuple-element.5, bf16[1,2,192,4096]{3,2,1,0:T(8,128)(2,1)S(1)} %copy-done.5), kind=kOutput, calls=%fused_computation.7 | convolution fusion | flops 1619001344 | bytes 27131904 | tf_op jit(solution)/shard_map/dot_general | solution.py:70
  367.8 0.0 reduce-scatter.2.cloned.1.call-update
  367.8 5.4 %fusion.1 = bf16[1,1,192,4096]{3,2,1,0:T(8,128)(2,1)S(1)} fusion(bf16[1024,192]{0,1:T(8,128)(2,1)S(1)} %get-tuple-element.6, bf16[1024,4096]{1,0:T(8,128)(2,1)} %bitcast.8), kind=kOutput, calls=%fused_computation.13 | convolution fusion | flops 1611399168 | bytes 10354688 | tf_op jit(solution)/shard_map/dot_general | solution.py:85
  373.2 0.0 copy-start.1
  373.2 5.8 %fusion.2 = bf16[1,1,192,4096]{3,2,1,0:T(8,128)(2,1)S(1)} fusion(bf16[1024,192]{0,1:T(8,128)(2,1)S(1)} %get-tuple-element.5, bf16[1024,4096]{1,0:T(8,128)(2,1)} %bitcast.8), kind=kOutput, calls=%fused_computation.14 | convolution fusion | flops 1611399168 | bytes 10354688 | tf_op jit(solution)/shard_map/dot_general | solution.py:86
  379.0 0.0 copy-start.8
  379.0 2.0 pad_maximum_fusion
  381.0 0.4 copy-done.2
  381.4 0.0 collective-permute-start
  381.4 5.3 %fusion.3 = bf16[1,192,4096]{2,1,0:T(8,128)(2,1)S(1)} fusion(bf16[1024,4096]{1,0:T(8,128)(2,1)} %bitcast.4, f32[1024,192]{0,1:T(8,128)S(1)} %copy-done.8, f32[1024,192]{0,1:T(8,128)S(1)} %fusion.6), kind=kOutput, calls=%fused_computation.15 | convolution fusion | flops 1612578816 | bytes 11534336 | tf_op jit(solution)/shard_map/dot_general | solution.py:89
  386.7 3.6 collective-permute-start.1
  390.4 92.2 %collective-permute-done.1 = bf16[1,192,4096]{2,1,0:T(8,128)(2,1)S(1)} collective-permute-done((bf16[1,192,4096]{2,1,0:T(8,128)(2,1)S(1)}, bf16[1,192,4096]{2,1,0:T(8,128)(2,1)S(1)}, u32[]{:S(2)}, u32[]{:S(2)}) %collective-permute-start.1) | collective-permute-done | bytes 1572896 | tf_op jit(solution)/shard_map/ppermute | solution.py:14
  482.6 1.7 add_convert_fusion.2
  484.3 8.8 %all-to-all-start.3 = ((bf16[16,64,512]{2,1,0:T(8,128)(2,1)}), bf16[16,64,512]{2,1,0:T(8,128)(2,1)S(1)}, u32[]{:S(2)}, u32[]{:S(2)}) async-start(bf16[16,64,512]{2,1,0:T(8,128)(2,1)} %reduce-scatter.2.cloned.1.call-done), calls=%async_computation.4 | async-start | bytes 2097152 | tf_op jit(solution)/shard_map/all_to_all | solution.py:77
  493.1 0.0 collective-permute-done
  493.1 5.8 %add_convert_fusion.1 = bf16[1,2,192,4096]{3,2,1,0:T(8,128)(2,1)} fusion(bf16[1,2,192,4096]{3,2,1,0:T(8,128)(2,1)} %collective-permute-done, bf16[1,1,192,4096]{3,2,1,0:T(8,128)(2,1)} %copy-done.2, bf16[1,1,192,4096]{3,2,1,0:T(8,128)(2,1)} %copy-done.1), kind=kLoop, calls=%fused_computation.9 | loop fusion | flops 7864320 | bytes 9437184 | tf_op jit(solution)/shard_map/convert_element_type | solution.py:94
  498.9 7.8 %all-to-all-done.3 = bf16[16,64,512]{2,1,0:T(8,128)(2,1)S(1)} async-done(((bf16[16,64,512]{2,1,0:T(8,128)(2,1)}), bf16[16,64,512]{2,1,0:T(8,128)(2,1)S(1)}, u32[]{:S(2)}, u32[]{:S(2)}) %all-to-all-start.3) | async-done | bytes 1048608 | tf_op jit(solution)/shard_map/all_to_all | solution.py:77
  506.8 2.0 gather_fusion.3
  508.7 0.1 gather.21
  508.9 1.3 reduce_sum.25
  (15 shorter events, 0.1 us)
Async XLA Ops:
  7.2 334.3 %copy-start = (bf16[1,192,4096]{2,1,0:T(8,128)(2,1)S(1)}, bf16[1,192,4096]{2,1,0:T(8,128)(2,1)}, u32[]{:S(2)}) copy-start(bf16[1,192,4096]{2,1,0:T(8,128)(2,1)} %param.11) | copy-start | bytes 4718596
  7.2 6.9 %copy-start.6 = (s32[128,4]{0,1:T(4,128)S(1)}, s32[128,4]{0,1:T(4,128)}, u32[]{:S(2)}) copy-start(s32[128,4]{0,1:T(4,128)} %param.8) | copy-start | bytes 6148
  7.2 8.9 %copy-start.7 = (bf16[128,4]{0,1:T(4,128)(2,1)S(1)}, bf16[128,4]{0,1:T(4,128)(2,1)}, u32[]{:S(2)}) copy-start(bf16[128,4]{0,1:T(4,128)(2,1)} %param.9) | copy-start | bytes 3076
  9.3 17.6 %all-to-all-start.1 = ((bf16[8,128,512]{2,1,0:T(8,128)(2,1)}), bf16[8,128,512]{2,1,0:T(8,128)(2,1)S(1)}, u32[]{:S(2)}, u32[]{:S(2)}) async-start(bf16[8,128,512]{2,1,0:T(8,128)(2,1)} %stack.8), calls=%async_computation.1 | async-start | bytes 2097152 | tf_op jit(solution)/shard_map/all_to_all | solution.py:41
  26.9 1.0 copy-start.3
  44.2 155.2 %all-to-all-start.2 = ((bf16[16,64,4096]{2,1,0:T(8,128)(2,1)}), bf16[16,64,4096]{2,1,0:T(8,128)(2,1)}, u32[]{:S(2)}, u32[]{:S(2)}) async-start(bf16[16,64,4096]{2,1,0:T(8,128)(2,1)} %broadcast_select_fusion), calls=%async_computation.2 | async-start | bytes 16777216 | tf_op jit(solution)/shard_map/all_to_all | solution.py:51
  52.1 26.8 %all-gather.2.cloned.1.call-start = ((), (), s32[]{:S(2)}) async-start(), calls=%async_computation.5 | async-start | bytes 1179648 | tf_op jit(solution)/shard_map/all_gather | solution.py:43
  199.4 142.1 %all-to-all-start = ((bf16[16,64,4096]{2,1,0:T(8,128)(2,1)}), bf16[16,64,4096]{2,1,0:T(8,128)(2,1)}, u32[]{:S(2)}, u32[]{:S(2)}) async-start(bf16[16,64,4096]{2,1,0:T(8,128)(2,1)} %fusion), calls=%async_computation | async-start | bytes 16777216 | tf_op jit(solution)/shard_map/all_to_all | solution.py:52
  207.8 276.5 %reduce-scatter.2.cloned.1.call-start = ((), (), s32[]{:S(2)}) async-start(), calls=%async_computation.6 | async-start | bytes 9437184 | tf_op jit(solution)/shard_map/reduce_scatter | solution.py:71
  208.0 6.9 %copy-start.4 = (bf16[1,2,192,4096]{3,2,1,0:T(8,128)(2,1)S(1)}, bf16[1,2,192,4096]{3,2,1,0:T(8,128)(2,1)}, u32[]{:S(2)}) copy-start(bf16[1,2,192,4096]{3,2,1,0:T(8,128)(2,1)} %param.10) | copy-start | bytes 9437188
  341.5 6.7 %copy-start.5 = (bf16[1,2,192,4096]{3,2,1,0:T(8,128)(2,1)S(1)}, bf16[1,2,192,4096]{3,2,1,0:T(8,128)(2,1)}, u32[]{:S(2)}) copy-start(bf16[1,2,192,4096]{3,2,1,0:T(8,128)(2,1)} %param.10) | copy-start | bytes 9437188
  373.2 5.8 %copy-start.1 = (bf16[1,1,192,4096]{3,2,1,0:T(8,128)(2,1)}, bf16[1,1,192,4096]{3,2,1,0:T(8,128)(2,1)S(1)}, u32[]{:S(2)}) copy-start(bf16[1,1,192,4096]{3,2,1,0:T(8,128)(2,1)S(1)} %fusion.1) | copy-start | bytes 4718596
  379.0 2.4 copy-start.2
  379.0 2.4 copy-start.8
  381.4 111.7 %collective-permute-start = (bf16[1,2,192,4096]{3,2,1,0:T(8,128)(2,1)}, bf16[1,2,192,4096]{3,2,1,0:T(8,128)(2,1)}, u32[]{:S(2)}, u32[]{:S(2)}) collective-permute-start(bf16[1,2,192,4096]{3,2,1,0:T(8,128)(2,1)} %pad_maximum_fusion), channel_id=1, source_target_pairs={{0,64},{64,0},{8,72},{72,8},{16,80},{80,16},{24,88},{88,24},{32,96... | collective-permute-start | bytes 9437192 | tf_op jit(solution)/shard_map/ppermute | solution.py:14
  386.7 95.8 %collective-permute-start.1 = (bf16[1,192,4096]{2,1,0:T(8,128)(2,1)S(1)}, bf16[1,192,4096]{2,1,0:T(8,128)(2,1)S(1)}, u32[]{:S(2)}, u32[]{:S(2)}) collective-permute-start(bf16[1,192,4096]{2,1,0:T(8,128)(2,1)S(1)} %fusion.3), channel_id=1, source_target_pairs={{0,64},{64,0},{8,72},{72,8},{16,80},{80,16},{24,88},{88,24},{32,96... | collective-permute-start | bytes 4718600 | tf_op jit(solution)/shard_map/ppermute | solution.py:14
  484.3 22.5 %all-to-all-start.3 = ((bf16[16,64,512]{2,1,0:T(8,128)(2,1)}), bf16[16,64,512]{2,1,0:T(8,128)(2,1)S(1)}, u32[]{:S(2)}, u32[]{:S(2)}) async-start(bf16[16,64,512]{2,1,0:T(8,128)(2,1)} %reduce-scatter.2.cloned.1.call-done), calls=%async_computation.4 | async-start | bytes 2097152 | tf_op jit(solution)/shard_map/all_to_all | solution.py:77
Sparse Core Ops, SparseCore 0:
  54.7 24.2 all-gather.1
  367.9 53.7 reduce-scatter.1
